TPU v7x, 256 devices: a whole 4x4x8 slice. The times are simulated.
256 devices in a mesh: blk: 32 (over x, z), uly: 4 (over y_hi, core), rep: 2 (over y_lo).
Axes of the slice: x: 4, y: 4 (y_hi: 2, y_lo: 2; y = y_hi * 2 + y_lo), z: 8, core: 2. Of those that a mesh axis runs over, the one named last changes fastest.
Arguments:
- queries: bfloat16 [2048, 3072], P(('rep', 'blk', 'uly')), parts along dimension 0, may hold values from -8 to 8
- keys_new: bfloat16 [2048, 3072], P(('rep', 'blk', 'uly')), parts along dimension 0, may hold values from -12 to 12
- values_new: bfloat16 [2048, 3072], P(('rep', 'blk', 'uly')), parts along dimension 0, may hold values from -6 to 6
- keys_cache: bfloat16 [14336, 3072], P(('rep', 'blk'), 'uly'), parts along dimension 0, may hold values from -12 to 12
- values_cache: bfloat16 [14336, 3072], P(('rep', 'blk'), 'uly'), parts along dimension 0, may hold values from -6 to 6
- query_frame: int32 [2048], P('rep'), parts along dimension 0, may hold values from 0 to 31, never falling along the last dimension, each value on 1 to 64 neighbouring positions
- context_frame: int32 [14336], P('rep'), parts along dimension 0, may hold values from 0 to 31, never falling along the last dimension, each value on 1 to 448 neighbouring positions
Outputs:
- attended: bfloat16 [2048, 3072], P(('rep', 'blk', 'uly')), parts along dimension 0
There are 2 independent parts, one for each index of `rep`. A program takes and returns all parts, laid end to end along the dimension named above; each array names one. Nothing has to cross between parts.
Inputs may be any that keep to these rules, and one draw needn't show every extreme that they name: `query_frame`: frame ids never fall along the group and every frame occurs. `context_frame`: frame ids never fall along the context and every frame occurs.
All inputs are finite; a program needn't handle non-finite values.
Results may differ from a plain program's by a relative error of at most 0.017.
Values may be sent and summed in bfloat16 or wider, within the bound.
A program may use at most 128 MiB of HBM per device.

v0:
```python
import jax
import jax.numpy as jnp
from jax import lax
from jax.sharding import PartitionSpec as P

HD = 128


def shards(queries, keys_new, values_new, keys_cache, values_cache, query_frame, context_frame):
    score_scale = HD ** (-0.5)
    heads_here = keys_cache.shape[1] // HD
    query_head, key_head, value_head = (
        lax.all_to_all(queries, "uly", split_axis=1, concat_axis=0, tiled=True),
        lax.all_to_all(keys_new, "uly", split_axis=1, concat_axis=0, tiled=True),
        lax.all_to_all(values_new, "uly", split_axis=1, concat_axis=0, tiled=True),
    )
    own_count = query_head.shape[0]
    cycle_size = lax.axis_size("blk")
    cycle_place = lax.axis_index("blk")
    frames_all = jnp.concatenate(
        [context_frame.reshape(cycle_size, -1), query_frame.reshape(cycle_size, -1)], 1
    ).reshape(-1)
    keys_here = jnp.concatenate([keys_cache, key_head], 0)
    values_here = jnp.concatenate([values_cache, value_head], 0)
    own_frames = lax.dynamic_slice_in_dim(query_frame, cycle_place * own_count, own_count, 0)
    query_split = query_head.reshape(own_count, heads_here, HD)
    highest = jnp.full((own_count, heads_here), -1e30, jnp.float32)
    key_piece = lax.all_gather(keys_here, "blk", axis=0, tiled=True)
    value_piece = lax.all_gather(values_here, "blk", axis=0, tiled=True)
    length = key_piece.shape[0]
    scores = (
        jnp.einsum(
            "qhd,khd->qhk",
            query_split,
            key_piece.reshape(length, heads_here, HD),
            preferred_element_type=jnp.float32,
        )
        * score_scale
    )
    visible = frames_all[None, None, :] <= own_frames[:, None, None]
    scores = jnp.where(visible, scores, jnp.float32(-1e30))
    raised = jnp.maximum(highest, jnp.max(scores, axis=2))
    weights = jnp.where(visible, jnp.exp(scores - raised[:, :, None]), jnp.float32(0.0))
    denominator = jnp.sum(weights, axis=2)
    summed = jnp.einsum(
        "qhk,khd->qhd",
        weights.astype(jnp.bfloat16),
        value_piece.reshape(length, heads_here, HD),
        preferred_element_type=jnp.float32,
    )
    highest, denominator, summed = (raised, denominator, summed)
    blended = (
        (summed / denominator[:, :, None]).reshape(own_count, heads_here * HD).astype(jnp.bfloat16)
    )
    return lax.all_to_all(blended, "uly", split_axis=0, concat_axis=1, tiled=True)


def solution(mesh):
    return jax.shard_map(
        shards,
        mesh=mesh,
        in_specs=(
            P(("rep", "blk", "uly"), None),
            P(("rep", "blk", "uly"), None),
            P(("rep", "blk", "uly"), None),
            P(("rep", "blk"), "uly"),
            P(("rep", "blk"), "uly"),
            P("rep"),
            P("rep"),
        ),
        out_specs=P(("rep", "blk", "uly"), None),
        check_vma=False,
    )
```

profile of v0, /device:TPU:1, one launch (start us, length us, event | category | flops | bytes accessed | tf_op | source)
XLA Modules:
  0.0 298.6 jit_solution(10287445708567107201)
XLA Ops:
  6.5 6.5 %all-to-all-start.1 = ((bf16[8,4,768]{2,0,1:T(8,128)(2,1)}), bf16[8,4,768]{2,0,1:T(8,128)(2,1)S(1)}, u32[]{:S(2)}, u32[]{:S(2)}) async-start(bf16[8,4,768]{2,0,1:T(8,128)(2,1)} %bitcast.36), calls=%async_computation.1 | async-start | bytes 98304 | tf_op jit(solution)/shard_map/all_to_all | solution.py:14
  13.0 0.0 all-gather.5.cloned.1.call-start
  13.0 1.1 copy.18
  14.2 3.6 %all-to-all-done.1 = bf16[8,4,768]{2,0,1:T(8,128)(2,1)S(1)} async-done(((bf16[8,4,768]{2,0,1:T(8,128)(2,1)}), bf16[8,4,768]{2,0,1:T(8,128)(2,1)S(1)}, u32[]{:S(2)}, u32[]{:S(2)}) %all-to-all-start.1) | async-done | bytes 49184 | tf_op jit(solution)/shard_map/all_to_all | solution.py:14
  17.7 0.2 copy.19
  17.9 1.0 pad_maximum_fusion.1
  18.9 0.0 all-gather.5.cloned.1.call-update
  18.9 4.1 %all-to-all-start = ((bf16[8,4,768]{2,0,1:T(8,128)(2,1)}), bf16[8,4,768]{2,0,1:T(8,128)(2,1)S(1)}, u32[]{:S(2)}, u32[]{:S(2)}) async-start(bf16[8,4,768]{2,0,1:T(8,128)(2,1)} %bitcast.37), calls=%async_computation | async-start | bytes 98304 | tf_op jit(solution)/shard_map/all_to_all | solution.py:15
  23.0 0.0 all-gather.3.cloned.1.call-start
  23.0 1.1 copy.16
  24.1 3.6 %all-to-all-done = bf16[8,4,768]{2,0,1:T(8,128)(2,1)S(1)} async-done(((bf16[8,4,768]{2,0,1:T(8,128)(2,1)}), bf16[8,4,768]{2,0,1:T(8,128)(2,1)S(1)}, u32[]{:S(2)}, u32[]{:S(2)}) %all-to-all-start) | async-done | bytes 49184 | tf_op jit(solution)/shard_map/all_to_all | solution.py:15
  27.7 0.2 copy.17
  27.9 0.9 pad_maximum_fusion
  28.8 0.0 all-gather.3.cloned.1.call-update
  28.8 4.1 %all-to-all-start.2 = ((bf16[8,4,768]{2,0,1:T(8,128)(2,1)}), bf16[8,4,768]{2,0,1:T(8,128)(2,1)S(1)}, u32[]{:S(2)}, u32[]{:S(2)}) async-start(bf16[8,4,768]{2,0,1:T(8,128)(2,1)} %bitcast.38), calls=%async_computation.2 | async-start | bytes 98304 | tf_op jit(solution)/shard_map/all_to_all | solution.py:13
  32.9 0.8 reshape.68
  33.7 0.8 dynamic_slice.3
  34.4 0.8 reshape.67
  35.3 0.1 add_bitcast_fusion
  35.4 0.2 broadcast_compare_fusion
  35.6 2.1 all-to-all-done.2
  37.7 0.1 reshape.70
  37.8 106.1 %all-gather.5.cloned.1.call-done = bf16[8192,768]{0,1:T(8,128)(2,1)} async-done(((bf16[256,768]{0,1:T(8,128)(2,1)}), bf16[8192,768]{0,1:T(8,128)(2,1)}) %all-gather.5.cloned.1.call-update) | async-done | bytes 12582928 | tf_op jit(solution)/shard_map/all_gather | solution.py:28
  143.8 6.0 %fusion.20 = (f32[32,6]{0,1:T(8,128)S(1)}, f32[32,6,8192]{2,0,1:T(8,128)S(1)}) fusion(bf16[8192,6,128]{0,2,1:T(8,128)(2,1)} %bitcast.30, bf16[32,6,128]{2,1,0:T(8,128)(2,1)S(1)} %reshape.70, pred[32,8192]{1,0:T(8,128)(4,1)S(1)} %broadcast_compare_fusion), kind=kOutput, calls=%fused_computation.20 | convolution fusion | flops 407371584 | bytes 19186432 | tf_op jit(solution)/shard_map/qhd,khd->qhk/dot_general | solution.py:32
  149.8 0.0 copy-start
  149.8 2.6 copy-done
  152.4 1.5 fusion.2
  153.9 116.4 %all-gather.3.cloned.1.call-done = bf16[8192,768]{0,1:T(8,128)(2,1)} async-done(((bf16[256,768]{0,1:T(8,128)(2,1)}), bf16[8192,768]{0,1:T(8,128)(2,1)}) %all-gather.3.cloned.1.call-update) | async-done | bytes 12582928 | tf_op jit(solution)/shard_map/all_gather | solution.py:29
  270.3 8.7 %fusion.15 = bf16[32,6,128]{2,0,1:T(8,128)(2,1)S(1)} fusion(bf16[8192,6,128]{0,2,1:T(8,128)(2,1)} %bitcast.39, f32[32,6,8192]{2,0,1:T(8,128)} %copy-done, f32[32,6]{0,1:T(8,128)S(1)} %broadcast_maximum_fusion, pred[32,8192]{1,0:T(8,128)(4,1)S(1)} %broadcast_compare_fusion, f32[32,6]{0,1:T(8,128)S(1)} %fusion.2), kind=kOutput, calls=%fused_computation.12 | convolution fusion | flops 407420928 | bytes 19187200 | tf_op jit(solution)/shard_map/qhk,khd->qhd/dot_general | solution.py:45
  279.1 0.1 convert_element_type.12
  279.2 11.9 %all_to_all.70 = bf16[4,8,768]{2,1,0:T(8,128)(2,1)S(1)} all-to-all(bf16[4,8,768]{2,1,0:T(8,128)(2,1)S(1)} %convert_element_type.12), channel_id=1, replica_groups=mesh['blk'=32,'uly'=4,'rep'=2] {'uly'}, dimensions={0} | all-to-all | bytes 98304 | tf_op jit(solution)/shard_map/all_to_all | solution.py:55
  291.1 0.6 copy.32
  (3 shorter events, 0.0 us)
Async XLA Ops:
  6.5 11.2 %all-to-all-start.1 = ((bf16[8,4,768]{2,0,1:T(8,128)(2,1)}), bf16[8,4,768]{2,0,1:T(8,128)(2,1)S(1)}, u32[]{:S(2)}, u32[]{:S(2)}) async-start(bf16[8,4,768]{2,0,1:T(8,128)(2,1)} %bitcast.36), calls=%async_computation.1 | async-start | bytes 98304 | tf_op jit(solution)/shard_map/all_to_all | solution.py:14
  13.0 130.8 %all-gather.5.cloned.1.call-start = ((), (), s32[]{:S(2)}) async-start(), calls=%async_computation.5 | async-start | bytes 12976128 | tf_op jit(solution)/shard_map/all_gather | solution.py:28
  18.9 8.8 %all-to-all-start = ((bf16[8,4,768]{2,0,1:T(8,128)(2,1)}), bf16[8,4,768]{2,0,1:T(8,128)(2,1)S(1)}, u32[]{:S(2)}, u32[]{:S(2)}) async-start(bf16[8,4,768]{2,0,1:T(8,128)(2,1)} %bitcast.37), calls=%async_computation | async-start | bytes 98304 | tf_op jit(solution)/shard_map/all_to_all | solution.py:15
  23.0 247.3 %all-gather.3.cloned.1.call-start = ((), (), s32[]{:S(2)}) async-start(), calls=%async_computation.4 | async-start | bytes 12976128 | tf_op jit(solution)/shard_map/all_gather | solution.py:29
  28.8 8.8 %all-to-all-start.2 = ((bf16[8,4,768]{2,0,1:T(8,128)(2,1)}), bf16[8,4,768]{2,0,1:T(8,128)(2,1)S(1)}, u32[]{:S(2)}, u32[]{:S(2)}) async-start(bf16[8,4,768]{2,0,1:T(8,128)(2,1)} %bitcast.38), calls=%async_computation.2 | async-start | bytes 98304 | tf_op jit(solution)/shard_map/all_to_all | solution.py:13
  149.8 2.6 copy-start
Sparse Core Ops, SparseCore 0:
  19.0 124.7 all-gather.4
  146.3 123.9 all-gather.2
where the time goes:
time: 299 us
  waiting for transfers between devices  232 us (78%)
  matrix products  14.7 us (5%)
  starting transfers between devices  14.6 us (5%)
  between operations  13.5 us (5%)
  blocking collectives  11.9 us (4%)
  local copies, waits for them, and re-layouts  8.38 us (3%)
  other arithmetic  3.72 us (1%)
    all_gather x1, waiting for transfers between devices, shards(): value_piece = lax.all_gather(values_here, 'blk', axis=0, tiled=True)  116 us
    all_gather x1, waiting for transfers between devices, shards(): key_piece = lax.all_gather(keys_here, 'blk', axis=0, tiled=True)  106 us
    all_to_all x1, blocking collectives, shards(): lax.all_to_all(blended, 'uly', split_axis=0, concat_axis=1, tiled=True)  11.9 us
    dot_general x1, matrix products, shards(): jnp.einsum('qhk,khd->qhd', weights.astype(jnp.bfloat16), value_piece.resh...  8.72 us
    all_to_all x1, starting transfers between devices, shards(): lax.all_to_all(keys_new, 'uly', split_axis=1, concat_axis=0, tiled=True)  6.48 us
  transfers between devices with their start and end apart: 5, of which 5 were waited for; matrix products, arithmetic and copies ran while one was open for 5% of the time, Pallas kernels for 0%

commit v1 on v0

v1 whole, which is shorter than its diff:
```python
import functools
import math

import jax
import jax.numpy as jnp
from jax import lax
from jax.experimental import pallas as pl
from jax.experimental.pallas import tpu as pltpu
from jax.sharding import PartitionSpec as P

HD = 128
NX, NZ, NU = 4, 8, 4
TOK = 8
CTXB = 224
NEWB = NU * TOK
KB = CTXB + NEWB
HEADS = 6
SCALE = math.log2(math.e) / math.sqrt(HD)
LOW = -1e30
MESH = pl.DeviceIdType.MESH
F32, BF16 = jnp.float32, jnp.bfloat16


def pair_start(x):
    return 3 * (x // 2) + lax.rem(x, 2)


def kernel(
    q_ref, kn_ref, vn_ref, kc_ref, vc_ref, qf_ref, cf_ref, out_ref,
    qland, nland, vland, qall, kbuf, vbuf, kt, vt, kft, qfr, osend, orecv, fsend, frecv,
    qs, qr, ns, nr, vs, vr, zs, zr, ks, kr, os, orr, fs, fr,
):
    blk, u = lax.axis_index("blk"), lax.axis_index("uly")
    x, z = blk // NZ, lax.rem(blk, NZ)
    me = x * NU + u
    slot_a = lax.rem(x, 2)
    slot_b = 1 - slot_a
    lane_a = pl.multiple_of(slot_a * HD, HD)
    lane_b = pl.multiple_of(slot_b * HD, HD)
    partner = NX - 1 - x

    def at(x_, z_, u_):
        return {"blk": x_ * NZ + z_, "uly": u_}

    def plane(i):
        dx, du = i // NU, i % NU
        return lax.rem(x + dx, NX), lax.rem(u + du, NU)

    def along(k):
        return at(x, lax.rem(z + NZ - k, NZ), u)

    barrier = pltpu.get_barrier_semaphore()
    for i in range(1, NX * NU):
        px, pu = plane(i)
        pl.semaphore_signal(barrier, inc=1, device_id=at(px, z, pu), device_id_type=MESH)
    for k in range(1, NZ):
        pl.semaphore_signal(barrier, inc=1, device_id=along(k), device_id_type=MESH)
    pl.semaphore_wait(barrier, NX * NU - 1 + NZ - 1)

    def columns(px, pu):
        return pl.ds(pl.multiple_of((HEADS * pu + pair_start(px)) * HD, HD), 2 * HD)

    def small(src, dst, ssem, rsem):
        copies = []
        for i in range(1, NX * NU):
            px, pu = plane(i)
            copies.append(
                pltpu.make_async_remote_copy(
                    src_ref=src.at[:, columns(px, pu)],
                    dst_ref=dst.at[me],
                    send_sem=ssem.at[i],
                    recv_sem=rsem.at[me],
                    device_id=at(px, z, pu),
                    device_id_type=MESH,
                )
            )
            copies[-1].start()
        pltpu.make_async_copy(src.at[:, columns(x, u)], dst.at[me], rsem.at[me]).start()
        return copies

    def landed(dst, rsem):
        for i in range(NX * NU):
            pltpu.make_async_copy(dst.at[i], dst.at[i], rsem.at[i]).wait()

    sends = small(q_ref, qland, qs, qr)

    def cache_cols(px, slot):
        return pl.ds(pl.multiple_of((pair_start(px) + slot) * HD, HD), HD)

    def cached(i, ref, buf, px, slot, dst, local):
        rows = buf.at[dst, pl.ds(0, CTXB)]
        src = ref.at[:, cache_cols(px, slot)]
        if local:
            pltpu.make_async_copy(src, rows, kr.at[i, dst]).start()
            return
        copy = pltpu.make_async_remote_copy(
            src_ref=src,
            dst_ref=rows,
            send_sem=ks.at[i, dst] if isinstance(dst, int) else ks.at[i, px],
            recv_sem=kr.at[i, dst],
            device_id=at(px, z, u),
            device_id_type=MESH,
        )
        copy.start()
        sends.append(copy)

    for i, (ref, buf) in enumerate(((kc_ref, kbuf), (vc_ref, vbuf))):
        cached(i, ref, buf, x, slot_b, 4, True)
        cached(i, ref, buf, partner, 1 - lax.rem(partner, 2), 5, False)
    for step in (2, 1, 3):
        px = lax.rem(x + step, NX)
        for i, (ref, buf) in enumerate(((kc_ref, kbuf), (vc_ref, vbuf))):
            cached(i, ref, buf, px, lax.rem(px, 2), x, False)
    for i, (ref, buf) in enumerate(((kc_ref, kbuf), (vc_ref, vbuf))):
        cached(i, ref, buf, x, slot_a, x, True)

    sends += small(kn_ref, nland, ns, nr)
    sends += small(vn_ref, vland, vs, vr)

    lane = lax.broadcasted_iota(jnp.int32, (1, 128), 1)
    for zz in range(NZ):
        row = jnp.zeros((1, 128), jnp.int32)
        for xx in range(NX):
            part = qf_ref[pl.ds(2 * xx + zz // 4, 1), :]
            part = pltpu.roll(part, (xx * 32 - (zz % 4) * 32) % 128, 1)
            row = jnp.where(lane // 32 == xx, part, row)
        qfr[zz] = jnp.broadcast_to(row, (8, 128))
    for xx in range(NX):
        place = (xx * NZ + z) * CTXB
        first, off = place // 128, lax.rem(place, 128)
        rows = [
            pltpu.roll(
                jnp.broadcast_to(cf_ref[pl.ds(jnp.minimum(first + j, 55), 1), :], (8, 128)),
                lax.rem(128 - off, 128),
                1,
            )
            for j in range(3)
        ]
        lanes8 = lax.broadcasted_iota(jnp.int32, (8, 128), 1)
        low = jnp.where(lanes8 < 128 - off, rows[0], rows[1])
        high = jnp.where(lanes8 < 128 - off, rows[1], rows[2])
        token = (xx * NZ + z) * NEWB
        new = jnp.broadcast_to(qf_ref[pl.ds(token // 128, 1), :], (8, 128))
        new = pltpu.roll(new, lax.rem(96 + 128 - lax.rem(token, 128), 128), 1)
        high = jnp.where(lanes8 >= 96, new, high)
        for h, part in enumerate((low, high)):
            wide = jnp.broadcast_to(part[:1].astype(F32), (128, 128))
            kft[xx, pl.ds(h * 128, 128), :] = wide.T.astype(jnp.int32)

    landed(qland, qr)
    for k in range(1, NZ):
        copy = pltpu.make_async_remote_copy(
            src_ref=qland,
            dst_ref=qall.at[k],
            send_sem=zs.at[k],
            recv_sem=zr.at[k],
            device_id=at(x, lax.rem(z + k, NZ), u),
            device_id_type=MESH,
        )
        copy.start()
        sends.append(copy)
    qall[0] = qland[...]

    landed(nland, nr)
    landed(vland, vr)

    def cache_landed(dst):
        for i, buf in enumerate((kbuf, vbuf)):
            rows = buf.at[dst, pl.ds(0, CTXB)]
            pltpu.make_async_copy(rows, rows, kr.at[i, dst]).wait()

    def join(dst, xx, lanes):
        for land, buf in ((nland, kbuf), (vland, vbuf)):
            new = land[pl.ds(xx * NU, NU), :, pl.ds(lanes, HD)]
            new = new.astype(F32).reshape(NEWB, HD).astype(BF16)
            buf[dst, pl.ds(CTXB, NEWB), :] = new
        vt[dst] = vbuf[dst].T

    def order(i):
        odd = lax.rem(i, 2)
        return odd * ((i + 1) // 2) + (1 - odd) * lax.rem(NZ - i // 2, NZ)

    def attend(head, blocks, lanes, i, wait):
        k = order(i)
        if wait:

            @pl.when(k > 0)
            def _():
                pltpu.make_async_copy(qall.at[k], qall.at[k], zr.at[k]).wait()

        zz = lax.rem(z + NZ - k, NZ)
        query = qall[k, :, :, pl.ds(lanes, HD)].astype(F32).reshape(NX * NU * TOK, HD)
        query = query.astype(BF16)
        frames = qfr[zz][:1]
        scores = []
        for dst, xx in blocks:
            s = lax.dot_general(
                kbuf[dst], query, (((1,), (1,)), ((), ())), preferred_element_type=F32
            )
            scores.append(jnp.where(kft[xx] <= frames, s * SCALE, LOW))
        top = functools.reduce(jnp.maximum, [jnp.max(s, axis=0, keepdims=True) for s in scores])
        total = jnp.zeros_like(top)
        summed = jnp.zeros((HD, 128), F32)
        for (dst, _), s in zip(blocks, scores):
            w = jnp.exp2(s - top)
            total += jnp.sum(w, axis=0, keepdims=True)
            summed += jnp.dot(vt[dst], w.astype(BF16), preferred_element_type=F32)
        osend[head, k, pl.ds(0, HD), :] = (summed / total).astype(BF16)
        level = top + jnp.log2(total)
        one = level.astype(BF16).astype(F32)
        two = (level - one).astype(BF16).astype(F32)
        three = level - one - two
        row = lax.broadcasted_iota(jnp.int32, (16, 128), 0)
        rows = jnp.where(row == 0, one, jnp.where(row == 1, two, jnp.where(row == 2, three, 0.0)))
        osend[head, k, pl.ds(HD, 16), :] = rows.astype(BF16)

        @pl.when(k > 0)
        def _():
            pltpu.make_async_remote_copy(
                src_ref=osend.at[head, k],
                dst_ref=orecv.at[head, k],
                send_sem=os.at[head, k],
                recv_sem=orr.at[head, k],
                device_id=along(k),
                device_id_type=MESH,
            ).start()

    cache_landed(4)
    cache_landed(5)
    join(4, x, lane_b)
    join(5, partner, lane_b)

    def shared(i, carry):
        attend(1, ((4, x), (5, partner)), lane_b, i, True)
        return carry

    lax.fori_loop(0, NZ, shared, 0)

    for xx in range(NX):
        cache_landed(xx)
        join(xx, xx, lane_a)

    def whole(i, carry):
        attend(0, tuple((xx, xx) for xx in range(NX)), lane_a, i, False)
        return carry

    lax.fori_loop(0, NZ, whole, 0)

    def merge(head):
        for k in range(1, NZ):
            pltpu.make_async_copy(orecv.at[head, k], orecv.at[head, k], orr.at[head, k]).wait()
        parts = [osend.at[head, 0]] + [orecv.at[head, k] for k in range(1, NZ)]
        levels = []
        for part in parts:
            tail = part[pl.ds(HD, 16), :].astype(F32)
            levels.append(tail[0:1] + tail[1:2] + tail[2:3])
        top = functools.reduce(jnp.maximum, levels)
        weights = [jnp.exp2(level - top) for level in levels]
        total = functools.reduce(jnp.add, weights)
        merged = jnp.zeros((HD, 128), F32)
        for part, w in zip(parts, weights):
            merged += part[pl.ds(0, HD), :].astype(F32) * w
        return merged / total, top + jnp.log2(total)

    merged, level = merge(1)
    fsend[:, pl.ds(TOK, TOK), :] = merged.T.reshape(NX * NU, TOK, HD)
    fsend[:, pl.ds(2 * TOK, TOK), :] = jnp.broadcast_to(level, (128, 128)).T.reshape(
        NX * NU, TOK, HD
    )
    merged, _ = merge(0)
    fsend[:, pl.ds(0, TOK), :] = merged.T.reshape(NX * NU, TOK, HD)

    for i in range(1, NX * NU):
        px, pu = plane(i)
        copy = pltpu.make_async_remote_copy(
            src_ref=fsend.at[px * NU + pu],
            dst_ref=frecv.at[me],
            send_sem=fs.at[i],
            recv_sem=fr.at[me],
            device_id=at(px, z, pu),
            device_id_type=MESH,
        )
        copy.start()
        sends.append(copy)
    pltpu.make_async_copy(fsend.at[me], frecv.at[me], fr.at[me]).start()
    landed(frecv, fr)
    for uu in range(NU):
        for half in range(2):
            ends = (frecv.at[2 * half * NU + uu], frecv.at[(2 * half + 1) * NU + uu])
            base = (HEADS * uu + 3 * half) * HD
            for e, end in enumerate(ends):
                out_ref[:, pl.ds(base + 2 * e * HD, HD)] = end[pl.ds(0, TOK), :].astype(BF16)
            levels = [end[pl.ds(2 * TOK, TOK), :] for end in ends]
            top = jnp.maximum(levels[0], levels[1])
            w = [jnp.exp2(level - top) for level in levels]
            both = [end[pl.ds(TOK, TOK), :] for end in ends]
            mixed = (both[0] * w[0] + both[1] * w[1]) / (w[0] + w[1])
            out_ref[:, pl.ds(base + HD, HD)] = mixed.astype(BF16)

    for copy in sends:
        copy.wait_send()
    for head in range(2):
        for k in range(1, NZ):
            pltpu.make_async_copy(osend.at[head, k], osend.at[head, k], os.at[head, k]).wait()


def shards(queries, keys_new, values_new, keys_cache, values_cache, query_frame, context_frame):
    anywhere = pl.BlockSpec(memory_space=pl.ANY)
    vmem = pl.BlockSpec(memory_space=pltpu.VMEM)
    dma = pltpu.SemaphoreType.DMA
    n = NX * NU
    return pl.pallas_call(
        kernel,
        out_shape=jax.ShapeDtypeStruct((TOK, queries.shape[1]), BF16),
        in_specs=[anywhere] * 5 + [vmem] * 2,
        out_specs=vmem,
        scratch_shapes=[
            pltpu.VMEM((n, TOK, 2 * HD), BF16),
            pltpu.VMEM((n, TOK, 2 * HD), BF16),
            pltpu.VMEM((n, TOK, 2 * HD), BF16),
            pltpu.VMEM((NZ, n, TOK, 2 * HD), BF16),
            pltpu.VMEM((6, KB, HD), BF16),
            pltpu.VMEM((6, KB, HD), BF16),
            pltpu.VMEM((1, 16, HD), BF16),
            pltpu.VMEM((6, HD, KB), BF16),
            pltpu.VMEM((NX, KB, 128), jnp.int32),
            pltpu.VMEM((NZ, 8, 128), jnp.int32),
            pltpu.VMEM((2, NZ, HD + 16, 128), BF16),
            pltpu.VMEM((2, NZ, HD + 16, 128), BF16),
            pltpu.VMEM((n, 3 * TOK, HD), F32),
            pltpu.VMEM((n, 3 * TOK, HD), F32),
            dma((n,)), dma((n,)), dma((n,)), dma((n,)), dma((n,)), dma((n,)),
            dma((NZ,)), dma((NZ,)),
            dma((2, 6)), dma((2, 6)),
            dma((2, NZ)), dma((2, NZ)),
            dma((n,)), dma((n,)),
        ],
        compiler_params=pltpu.CompilerParams(
            collective_id=0, has_side_effects=True, vmem_limit_bytes=48 * 2**20
        ),
    )(
        queries, keys_new, values_new, keys_cache, values_cache,
        query_frame.reshape(8, 128), context_frame.reshape(56, 128),
    )


def solution(mesh):
    return jax.shard_map(
        shards,
        mesh=mesh,
        in_specs=(
            P(("rep", "blk", "uly"), None),
            P(("rep", "blk", "uly"), None),
            P(("rep", "blk", "uly"), None),
            P(("rep", "blk"), "uly"),
            P(("rep", "blk"), "uly"),
            P("rep"),
            P("rep"),
        ),
        out_specs=P(("rep", "blk", "uly"), None),
        check_vma=False,
    )
```

time: 299 us -> 60.9 us (0.20)
  waiting for transfers between devices: 232 us -> 0 us
  Pallas kernels: 0 us -> 54 us
  matrix products: 14.7 us -> 0 us
  starting transfers between devices: 14.6 us -> 0 us
  between operations: 13.5 us -> 0.02 us
  blocking collectives: 11.9 us -> 0 us
  other arithmetic: 3.72 us -> 0 us
    all_gather x2 -> x0, waiting for transfers between devices: 222 us -> none  [the longest x1 116 us: shards(): value_piece = lax.all_gather(values_here, 'blk', axis=0, tiled=True)]
    pallas_call x0 -> x1, Pallas kernels: none -> 54 us  [shards(): pl.pallas_call(kernel, out_shape=jax.ShapeDtypeStruct((TOK, queries.shape...]
    dot_general x2 -> x0, matrix products: 14.7 us -> none  [the longest x1 8.72 us: shards(): jnp.einsum('qhk,khd->qhd', weights.astype(jnp.bfloat16), value_piece.resh...]
    all_to_all x3 -> x0, starting transfers between devices: 14.6 us -> none  [the longest x1 6.48 us: shards(): lax.all_to_all(keys_new, 'uly', split_axis=1, concat_axis=0, tiled=True)]
    all_to_all x1 -> x0, blocking collectives: 11.9 us -> none  [shards(): lax.all_to_all(blended, 'uly', split_axis=0, concat_axis=1, tiled=True)]
    all_to_all x3 -> x0, waiting for transfers between devices: 9.25 us -> none  [the longest x1 3.57 us: shards(): lax.all_to_all(keys_new, 'uly', split_axis=1, concat_axis=0, tiled=True)]
    unnamed x6 -> x15, local copies, waits for them, and re-layouts: 5.53 us -> 6.41 us
  transfers between devices with their start and end apart: 5 -> 0, of which waited for: 5 -> 0; matrix products, arithmetic and copies ran while one was open for 5% -> 0% of each run, Pallas kernels for 0% -> 0%
where the time goes in v1:
time: 60.9 us; the launch traced here: 60.5 us
  Pallas kernels  54 us (89%)
  local copies, waits for them, and re-layouts  6.41 us (11%)
    pallas_call x1, Pallas kernels, shards(): pl.pallas_call(kernel, out_shape=jax.ShapeDtypeStruct((TOK, queries.shape...  54 us
    unnamed x15, local copies, waits for them, and re-layouts  6.41 us

profile of v1, /device:TPU:1, one launch (start us, length us, event | category | flops | bytes accessed | tf_op | source)
XLA Modules:
  0.0 60.5 jit_solution(520958757771312317)
XLA Ops:
  0.0 0.0 copy-start
  0.0 1.0 %copy-done = bf16[224,768]{1,0:T(8,128)(2,1)S(1)} copy-done((bf16[224,768]{1,0:T(8,128)(2,1)S(1)}, bf16[224,768]{1,0:T(8,128)(2,1)}, u32[]{:S(2)}) %copy-start) | copy-done | bytes 344088
  1.0 0.0 copy-start.1
  1.0 1.0 %copy-done.1 = bf16[224,768]{1,0:T(8,128)(2,1)S(1)} copy-done((bf16[224,768]{1,0:T(8,128)(2,1)S(1)}, bf16[224,768]{1,0:T(8,128)(2,1)}, u32[]{:S(2)}) %copy-start.1) | copy-done | bytes 344088
  2.0 0.0 copy-start.2
  2.0 0.8 %copy-done.2 = bf16[8,3072]{1,0:T(8,128)(2,1)S(1)} copy-done((bf16[8,3072]{1,0:T(8,128)(2,1)S(1)}, bf16[8,3072]{1,0:T(8,128)(2,1)}, u32[]{:S(2)}) %copy-start.2) | copy-done | bytes 49176
  2.8 0.0 copy-start.3
  2.8 0.8 %copy-done.3 = bf16[8,3072]{1,0:T(8,128)(2,1)S(1)} copy-done((bf16[8,3072]{1,0:T(8,128)(2,1)S(1)}, bf16[8,3072]{1,0:T(8,128)(2,1)}, u32[]{:S(2)}) %copy-start.3) | copy-done | bytes 49176
  3.6 0.0 copy-start.4
  3.6 0.8 %copy-done.4 = bf16[8,3072]{1,0:T(8,128)(2,1)S(1)} copy-done((bf16[8,3072]{1,0:T(8,128)(2,1)S(1)}, bf16[8,3072]{1,0:T(8,128)(2,1)}, u32[]{:S(2)}) %copy-start.4) | copy-done | bytes 49176
  4.4 0.0 copy-start.5
  4.4 0.7 %copy-done.5 = s32[7168]{0:T(1024)S(1)} copy-done((s32[7168]{0:T(1024)S(1)}, s32[7168]{0:T(1024)}, u32[]{:S(2)}) %copy-start.5) | copy-done | bytes 28696
  5.1 0.0 copy-start.6
  5.1 0.7 %copy-done.6 = s32[1024]{0:T(1024)S(1)} copy-done((s32[1024]{0:T(1024)S(1)}, s32[1024]{0:T(1024)}, u32[]{:S(2)}) %copy-start.6) | copy-done | bytes 4120
  5.8 54.0 %shard_map.73 = bf16[8,3072]{1,0:T(8,128)(2,1)S(1)} custom-call(bf16[8,3072]{1,0:T(8,128)(2,1)S(1)} %copy-done.2, bf16[8,3072]{1,0:T(8,128)(2,1)S(1)} %copy-done.3, bf16[8,3072]{1,0:T(8,128)(2,1)S(1)} %copy-done.4, bf16[224,768]{1,0:T(8,128)(2,1)S(1)} %copy-done, bf16[224,768]{1,0:T(8,128)(2,1)S(1)} %copy-done.1, s32[8,128]{1,0:T(8,128)S(1)} %bitcast.3, ...), custom_call_target="tpu_custom_call" | custom-call | tf_op jit(solution)/shard_map/pallas_call | solution.py:312
  59.8 0.6 %copy.9 = bf16[8,3072]{1,0:T(8,128)(2,1)} copy(bf16[8,3072]{1,0:T(8,128)(2,1)S(1)} %shard_map.73) | data formatting | bytes 98304
Async XLA Ops:
  0.0 1.0 %copy-start = (bf16[224,768]{1,0:T(8,128)(2,1)S(1)}, bf16[224,768]{1,0:T(8,128)(2,1)}, u32[]{:S(2)}) copy-start(bf16[224,768]{1,0:T(8,128)(2,1)} %kc_ref.1) | copy-start | bytes 1032196
  1.0 1.0 %copy-start.1 = (bf16[224,768]{1,0:T(8,128)(2,1)S(1)}, bf16[224,768]{1,0:T(8,128)(2,1)}, u32[]{:S(2)}) copy-start(bf16[224,768]{1,0:T(8,128)(2,1)} %vc_ref.1) | copy-start | bytes 1032196
  2.0 0.8 %copy-start.2 = (bf16[8,3072]{1,0:T(8,128)(2,1)S(1)}, bf16[8,3072]{1,0:T(8,128)(2,1)}, u32[]{:S(2)}) copy-start(bf16[8,3072]{1,0:T(8,128)(2,1)} %q_ref.1) | copy-start | bytes 147460
  2.8 0.8 %copy-start.3 = (bf16[8,3072]{1,0:T(8,128)(2,1)S(1)}, bf16[8,3072]{1,0:T(8,128)(2,1)}, u32[]{:S(2)}) copy-start(bf16[8,3072]{1,0:T(8,128)(2,1)} %kn_ref.1) | copy-start | bytes 147460
  3.6 0.8 %copy-start.4 = (bf16[8,3072]{1,0:T(8,128)(2,1)S(1)}, bf16[8,3072]{1,0:T(8,128)(2,1)}, u32[]{:S(2)}) copy-start(bf16[8,3072]{1,0:T(8,128)(2,1)} %vn_ref.1) | copy-start | bytes 147460
  4.4 0.7 %copy-start.5 = (s32[7168]{0:T(1024)S(1)}, s32[7168]{0:T(1024)}, u32[]{:S(2)}) copy-start(s32[7168]{0:T(1024)} %param.13) | copy-start | bytes 86020
  5.1 0.7 %copy-start.6 = (s32[1024]{0:T(1024)S(1)}, s32[1024]{0:T(1024)}, u32[]{:S(2)}) copy-start(s32[1024]{0:T(1024)} %param.12) | copy-start | bytes 12292

commit v2 on v1

v2 whole, which is shorter than its diff:
```python
import functools
import math

import jax
import jax.numpy as jnp
from jax import lax
from jax.experimental import pallas as pl
from jax.experimental.pallas import tpu as pltpu
from jax.sharding import PartitionSpec as P

HD = 128
NX, NZ, NU = 4, 8, 4
TOK = 8
CTXB = 224
NEWB = NU * TOK
KB = CTXB + NEWB
HEADS = 6
SCALE = math.log2(math.e) / math.sqrt(HD)
LOW = -1e30
MESH = pl.DeviceIdType.MESH
F32, BF16 = jnp.float32, jnp.bfloat16


def pair_start(x):
    return 3 * (x // 2) + lax.rem(x, 2)


def kernel(
    q_ref, kn_ref, vn_ref, kc_ref, vc_ref, qf_hbm, cf_hbm, out_ref,
    qf_ref, cf_ref,    qland, nland, vland, npair, vpair, qall, kbuf, vbuf, vt, sbuf, kft, qfr, osend, orecv, fsend, frecv,
    fr_sem, qs, qr, ns, nr, vs, vr, zs, zr, ps, pr, ks, kr, os, orr, fs, fr,
):
    blk, u = lax.axis_index("blk"), lax.axis_index("uly")
    x, z = blk // NZ, lax.rem(blk, NZ)
    me = x * NU + u
    slot = lax.rem(z, 2)
    lane = pl.multiple_of(slot * HD, HD)
    other = z + 1 - 2 * slot
    base = z - slot
    even = lax.rem(x + z, 2) == 0
    role = lax.rem(x + z, 2)

    def at(x_, z_, u_):
        return {"blk": x_ * NZ + z_, "uly": u_}

    def plane(i):
        dx, du = i // NU, i % NU
        return lax.rem(x + dx, NX), lax.rem(u + du, NU)

    def along(k):
        return at(x, lax.rem(z + NZ - k, NZ), u)

    frame_copies = [
        pltpu.make_async_copy(qf_hbm, qf_ref, fr_sem.at[0]),
        pltpu.make_async_copy(cf_hbm, cf_ref, fr_sem.at[1]),
    ]
    for copy in frame_copies:
        copy.start()

    barrier = pltpu.get_barrier_semaphore()
    for i in range(1, NX * NU):
        px, pu = plane(i)
        pl.semaphore_signal(barrier, inc=1, device_id=at(px, z, pu), device_id_type=MESH)
    for k in range(1, NZ):
        pl.semaphore_signal(barrier, inc=1, device_id=along(k), device_id_type=MESH)
    for step in range(1, NX):
        pl.semaphore_signal(
            barrier, inc=1, device_id=at(lax.rem(x + step, NX), other, u), device_id_type=MESH
        )
    pl.semaphore_wait(barrier, NX * NU - 1 + NZ - 1 + NX - 1)

    def columns(px, pu):
        return pl.ds(pl.multiple_of((HEADS * pu + pair_start(px)) * HD, HD), 2 * HD)

    def small(src, dst, ssem, rsem):
        copies = []
        for i in range(1, NX * NU):
            px, pu = plane(i)
            copies.append(
                pltpu.make_async_remote_copy(
                    src_ref=src.at[:, columns(px, pu)],
                    dst_ref=dst.at[me],
                    send_sem=ssem.at[i],
                    recv_sem=rsem.at[me],
                    device_id=at(px, z, pu),
                    device_id_type=MESH,
                )
            )
            copies[-1].start()
        pltpu.make_async_copy(src.at[:, columns(x, u)], dst.at[me], rsem.at[me]).start()
        return copies

    def landed(dst, rsem):
        for i in range(NX * NU):
            pltpu.make_async_copy(dst.at[i], dst.at[i], rsem.at[i]).wait()

    sends = small(q_ref, qland, qs, qr)

    caches = ((0, kc_ref, kbuf), (1, vc_ref, vbuf))

    def cached(px, pz, ssem):
        mine = lax.rem(z, 2)
        whole = lax.rem(px + pz, 2) == 0
        far = (x != px).astype(jnp.int32)
        dst = jnp.where(whole, mine * NX + x, mine * 2 + far)
        copies = []
        for i, ref, buf in caches:
            src = ref.at[:, pl.ds(pl.multiple_of((pair_start(px) + lax.rem(pz, 2)) * HD, HD), HD)]
            copies.append(
                pltpu.make_async_remote_copy(
                    src_ref=src,
                    dst_ref=buf.at[dst, pl.ds(0, CTXB)],
                    send_sem=ks.at[i, ssem],
                    recv_sem=kr.at[i, dst],
                    device_id=at(px, pz, u),
                    device_id_type=MESH,
                )
            )
        return copies

    def takes(px, pz):
        return (lax.rem(px + pz, 2) == 0) | (px == x) | (px == NX - 1 - x)

    for step in (2, 1, 3, 0):
        px = lax.rem(x + step, NX)
        for n, pz in enumerate((other, z)):
            if step == 0 and n == 1:
                continue

            @pl.when(takes(px, pz))
            def _():
                for copy in cached(px, pz, 2 * step + n):
                    copy.start()

    own_slot = jnp.where(even, slot * NX + x, slot * 2)
    for i, ref, buf in caches:
        pltpu.make_async_copy(
            ref.at[:, pl.ds(pl.multiple_of((pair_start(x) + slot) * HD, HD), HD)],
            buf.at[own_slot, pl.ds(0, CTXB)],
            kr.at[i, own_slot],
        ).start()

    sends += small(kn_ref, nland, ns, nr)
    sends += small(vn_ref, vland, vs, vr)

    for copy in frame_copies:
        copy.wait()
    lanes = lax.broadcasted_iota(jnp.int32, (1, 128), 1)
    for zz in range(NZ):
        row = jnp.zeros((1, 128), jnp.int32)
        for xx in range(NX):
            part = qf_ref[pl.ds(2 * xx + zz // 4, 1), :]
            part = pltpu.roll(part, (xx * 32 - (zz % 4) * 32) % 128, 1)
            row = jnp.where(lanes // 32 == xx, part, row)
        qfr[zz] = jnp.broadcast_to(row, (8, 128))
    for block in range(2 * NX):
        xx, bz = block % NX, base + block // NX
        place = (xx * NZ + bz) * CTXB
        first, off = place // 128, lax.rem(place, 128)
        rows = [
            pltpu.roll(
                jnp.broadcast_to(cf_ref[pl.ds(jnp.minimum(first + j, 55), 1), :], (8, 128)),
                lax.rem(128 - off, 128),
                1,
            )
            for j in range(3)
        ]
        lanes8 = lax.broadcasted_iota(jnp.int32, (8, 128), 1)
        low = jnp.where(lanes8 < 128 - off, rows[0], rows[1])
        high = jnp.where(lanes8 < 128 - off, rows[1], rows[2])
        token = (xx * NZ + bz) * NEWB
        new = jnp.broadcast_to(qf_ref[pl.ds(token // 128, 1), :], (8, 128))
        new = pltpu.roll(new, lax.rem(96 + 128 - lax.rem(token, 128), 128), 1)
        high = jnp.where(lanes8 >= 96, new, high)
        for h, part in enumerate((low, high)):
            wide = jnp.broadcast_to(part[:1].astype(F32), (128, 128))
            kft[block, pl.ds(h * 128, 128), :] = wide.T.astype(jnp.int32)

    landed(qland, qr)
    for k in (1, 7, 2, 6, 3, 5, 4):
        pz = lax.rem(z + k, NZ)
        copy = pltpu.make_async_remote_copy(
            src_ref=qland.at[:, :, pl.ds(pl.multiple_of(lax.rem(pz, 2) * HD, HD), HD)],
            dst_ref=qall.at[k],
            send_sem=zs.at[k],
            recv_sem=zr.at[k],
            device_id=at(x, pz, u),
            device_id_type=MESH,
        )
        copy.start()
        sends.append(copy)
    qall[0] = qland[:, :, pl.ds(lane, HD)]

    landed(nland, nr)
    landed(vland, vr)
    lands = ((0, nland, npair, kbuf), (1, vland, vpair, vbuf))
    for i, land, pair, _ in lands:
        copy = pltpu.make_async_remote_copy(
            src_ref=land.at[:, :, pl.ds(pl.multiple_of((1 - slot) * HD, HD), HD)],
            dst_ref=pair,
            send_sem=ps.at[i],
            recv_sem=pr.at[i],
            device_id=at(x, other, u),
            device_id_type=MESH,
        )
        copy.start()
        sends.append(copy)
    for i, _, pair, _ in lands:
        pltpu.make_async_copy(pair, pair, pr.at[i]).wait()

    def join(dst, xx, mine):
        for i, land, pair, buf in lands:
            rows = buf.at[dst, pl.ds(0, CTXB)]
            pltpu.make_async_copy(rows, rows, kr.at[i, dst]).wait()
            here = land[pl.ds(xx * NU, NU), :, pl.ds(lane, HD)]
            there = pair[pl.ds(xx * NU, NU)]
            new = jnp.where(mine, here.astype(F32), there.astype(F32))
            buf[dst, pl.ds(CTXB, NEWB), :] = new.reshape(NEWB, HD).astype(BF16)
        vt[dst] = vbuf[dst].T

    def order(i):
        odd = lax.rem(i, 2)
        return odd * ((i + 1) // 2) + (1 - odd) * lax.rem(NZ - i // 2, NZ)

    def attend(blocks, i):
        k = order(i)

        @pl.when(k > 0)
        def _():
            pltpu.make_async_copy(qall.at[k], qall.at[k], zr.at[k]).wait()

        zz = lax.rem(z + NZ - k, NZ)
        query = qall[k].astype(F32).reshape(NX * NU * TOK, HD).astype(BF16)
        frames = qfr[zz][:1]
        top = jnp.full((8, 128), LOW, F32)
        for dst, block in blocks:
            s = lax.dot_general(
                kbuf[dst], query, (((1,), (1,)), ((), ())), preferred_element_type=F32
            )
            s = jnp.where(kft[block] <= frames, s * SCALE, LOW)
            sbuf[dst] = s
            top = jnp.maximum(top, jnp.max(s.reshape(KB // 8, 8, 128), axis=0))
        top = jnp.max(top, axis=0, keepdims=True)
        total = jnp.zeros((8, 128), F32)
        summed = jnp.zeros((HD, 128), F32)
        for dst, _ in blocks:
            w = jnp.exp2(sbuf[dst] - top)
            total += jnp.sum(w.reshape(KB // 8, 8, 128), axis=0)
            summed += jnp.dot(vt[dst], w.astype(BF16), preferred_element_type=F32)
        total = jnp.sum(total, axis=0, keepdims=True)
        osend[k, pl.ds(0, HD), :] = (summed / total).astype(BF16)
        level = top + jnp.log2(total)
        one = level.astype(BF16).astype(F32)
        two = (level - one).astype(BF16).astype(F32)
        three = level - one - two
        row = lax.broadcasted_iota(jnp.int32, (16, 128), 0)
        rows = jnp.where(row == 0, one, jnp.where(row == 1, two, jnp.where(row == 2, three, 0.0)))
        osend[k, pl.ds(HD, 16), :] = rows.astype(BF16)

        @pl.when(k > 0)
        def _():
            pltpu.make_async_remote_copy(
                src_ref=osend.at[k],
                dst_ref=orecv.at[k],
                send_sem=os.at[k],
                recv_sem=orr.at[k],
                device_id=along(k),
                device_id_type=MESH,
            ).start()

    def work(blocks):
        for dst, block in blocks:
            xx = lax.rem(block, NX)
            join(dst, xx, block // NX == slot)

        def chunk(i, carry):
            attend(blocks, i)
            return carry

        lax.fori_loop(0, NZ, chunk, 0)

    @pl.when(even)
    def _():
        work([(b, b) for b in range(2 * NX)])

    @pl.when(jnp.logical_not(even))
    def _():
        work([(2 * b + f, b * NX + (x if f == 0 else NX - 1 - x)) for b in range(2) for f in range(2)])

    orecv[0] = osend[0]

    for k in range(1, NZ):
        pltpu.make_async_copy(orecv.at[k], orecv.at[k], orr.at[k]).wait()

    def merge(kind):
        parity = lax.rem(role + kind, 2)
        parts = [orecv.at[2 * j + parity] for j in range(NZ // 2)]
        levels = []
        for part in parts:
            tail = part[pl.ds(HD, 16), :].astype(F32)
            levels.append(tail[0:1] + tail[1:2] + tail[2:3])
        top = functools.reduce(jnp.maximum, levels)
        weights = [jnp.exp2(level - top) for level in levels]
        total = functools.reduce(jnp.add, weights)
        merged = jnp.zeros((HD, 128), F32)
        for part, w in zip(parts, weights):
            merged += part[pl.ds(0, HD), :].astype(F32) * w
        return merged / total, top + jnp.log2(total)

    merged, level = merge(1)
    fsend[:, pl.ds(TOK, TOK), :] = merged.T.reshape(NX * NU, TOK, HD)
    fsend[:, pl.ds(2 * TOK, TOK), :] = jnp.broadcast_to(level, (128, 128)).T.reshape(
        NX * NU, TOK, HD
    )
    merged, _ = merge(0)
    fsend[:, pl.ds(0, TOK), :] = merged.T.reshape(NX * NU, TOK, HD)

    for i in range(1, NX * NU):
        px, pu = plane(i)
        copy = pltpu.make_async_remote_copy(
            src_ref=fsend.at[px * NU + pu],
            dst_ref=frecv.at[me],
            send_sem=fs.at[i],
            recv_sem=fr.at[me],
            device_id=at(px, z, pu),
            device_id_type=MESH,
        )
        copy.start()
        sends.append(copy)
    pltpu.make_async_copy(fsend.at[me], frecv.at[me], fr.at[me]).start()
    landed(frecv, fr)
    for uu in range(NU):
        for half in range(2):
            ends = (frecv.at[2 * half * NU + uu], frecv.at[(2 * half + 1) * NU + uu])
            base = (HEADS * uu + 3 * half) * HD
            for e, end in enumerate(ends):
                out_ref[:, pl.ds(base + 2 * e * HD, HD)] = end[pl.ds(0, TOK), :].astype(BF16)
            levels = [end[pl.ds(2 * TOK, TOK), :] for end in ends]
            top = jnp.maximum(levels[0], levels[1])
            w = [jnp.exp2(level - top) for level in levels]
            both = [end[pl.ds(TOK, TOK), :] for end in ends]
            mixed = (both[0] * w[0] + both[1] * w[1]) / (w[0] + w[1])
            out_ref[:, pl.ds(base + HD, HD)] = mixed.astype(BF16)

    for copy in sends:
        copy.wait_send()
    for step in range(NX):
        px = lax.rem(x + step, NX)
        for n, pz in enumerate((other, z)):
            if step == 0 and n == 1:
                continue

            @pl.when(takes(px, pz))
            def _():
                for copy in cached(px, pz, 2 * step + n):
                    copy.wait_send()

    for k in range(1, NZ):
        pltpu.make_async_copy(osend.at[k], osend.at[k], os.at[k]).wait()


def shards(queries, keys_new, values_new, keys_cache, values_cache, query_frame, context_frame):
    hbm = pl.BlockSpec(memory_space=pltpu.HBM)
    vmem = pl.BlockSpec(memory_space=pltpu.VMEM)
    dma = pltpu.SemaphoreType.DMA
    n = NX * NU
    return pl.pallas_call(
        kernel,
        out_shape=jax.ShapeDtypeStruct((TOK, queries.shape[1]), BF16),
        in_specs=[hbm] * 7,
        out_specs=vmem,
        scratch_shapes=[
            pltpu.VMEM((8, 128), jnp.int32),
            pltpu.VMEM((56, 128), jnp.int32),
            pltpu.VMEM((n, TOK, 2 * HD), BF16),
            pltpu.VMEM((n, TOK, 2 * HD), BF16),
            pltpu.VMEM((n, TOK, 2 * HD), BF16),
            pltpu.VMEM((n, TOK, HD), BF16),
            pltpu.VMEM((n, TOK, HD), BF16),
            pltpu.VMEM((NZ, n, TOK, HD), BF16),
            pltpu.VMEM((2 * NX, KB, HD), BF16),
            pltpu.VMEM((2 * NX, KB, HD), BF16),
            pltpu.VMEM((2 * NX, HD, KB), BF16),
            pltpu.VMEM((2 * NX, KB, 128), F32),
            pltpu.VMEM((2 * NX, KB, 128), jnp.int32),
            pltpu.VMEM((NZ, 8, 128), jnp.int32),
            pltpu.VMEM((NZ, HD + 16, 128), BF16),
            pltpu.VMEM((NZ, HD + 16, 128), BF16),
            pltpu.VMEM((n, 3 * TOK, HD), F32),
            pltpu.VMEM((n, 3 * TOK, HD), F32),
            dma((2,)),
            dma((n,)), dma((n,)), dma((n,)), dma((n,)), dma((n,)), dma((n,)),
            dma((NZ,)), dma((NZ,)),
            dma((2,)), dma((2,)),
            dma((2, 2 * NX)), dma((2, 2 * NX)),
            dma((NZ,)), dma((NZ,)),
            dma((n,)), dma((n,)),
        ],
        compiler_params=pltpu.CompilerParams(
            collective_id=0, has_side_effects=True, vmem_limit_bytes=64 * 2**20
        ),
    )(
        queries, keys_new, values_new, keys_cache, values_cache,
        query_frame.reshape(8, 128), context_frame.reshape(56, 128),
    )


def solution(mesh):
    return jax.shard_map(
        shards,
        mesh=mesh,
        in_specs=(
            P(("rep", "blk", "uly"), None),
            P(("rep", "blk", "uly"), None),
            P(("rep", "blk", "uly"), None),
            P(("rep", "blk"), "uly"),
            P(("rep", "blk"), "uly"),
            P("rep"),
            P("rep"),
        ),
        out_specs=P(("rep", "blk", "uly"), None),
        check_vma=False,
    )
```

time: 60.9 us -> 51.9 us (0.85)
  local copies, waits for them, and re-layouts: 6.41 us -> 1.42 us
  Pallas kernels: 54 us -> 50.3 us
    unnamed x15 -> x1, local copies, waits for them, and re-layouts: 6.41 us -> 1.42 us
    pallas_call x1, Pallas kernels: 54 us -> 50.3 us  [shards(): pl.pallas_call(kernel, out_shape=jax.ShapeDtypeStruct((TOK, queries.shape...]
where the time goes in v2:
time: 51.9 us; the launch traced here: 51.8 us
  Pallas kernels  50.3 us (97%)
  local copies, waits for them, and re-layouts  1.42 us (3%)
    pallas_call x1, Pallas kernels, shards(): pl.pallas_call(kernel, out_shape=jax.ShapeDtypeStruct((TOK, queries.shape...  50.3 us
    unnamed x1, local copies, waits for them, and re-layouts  1.42 us

profile of v2, /device:TPU:1, one launch (start us, length us, event | category | flops | bytes accessed | tf_op | source)
XLA Modules:
  0.0 51.8 jit_solution(18415788825850326605)
XLA Ops:
  0.0 50.3 %shard_map.73 = bf16[8,3072]{1,0:T(8,128)(2,1)} custom-call(bf16[8,3072]{1,0:T(8,128)(2,1)} %q_ref.1, bf16[8,3072]{1,0:T(8,128)(2,1)} %kn_ref.1, bf16[8,3072]{1,0:T(8,128)(2,1)} %vn_ref.1, bf16[224,768]{1,0:T(8,128)(2,1)} %kc_ref.1, bf16[224,768]{1,0:T(8,128)(2,1)} %vc_ref.1, s32[8,128]{1,0:T(8,128)} %bitcast.3, s32[56,128]{1,0:T(8,128)} %bitcast.2), custom_call_target="tpu_custom_call" | custom-call | tf_op jit(solution)/shard_map/pallas_call | solution.py:367
  50.3 1.4 %copy.9 = bf16[8,3072]{1,0:T(8,128)(2,1)} copy(bf16[8,3072]{1,0:T(8,128)(2,1)} %shard_map.73) | data formatting | bytes 98304

commit v3 on v2

--- a/solution.py
+++ b/solution.py
@@ -27,14 +27,13 @@
 
 def kernel(
     q_ref, kn_ref, vn_ref, kc_ref, vc_ref, qf_hbm, cf_hbm, out_ref,
-    qf_ref, cf_ref,    qland, nland, vland, npair, vpair, qall, kbuf, vbuf, vt, sbuf, kft, qfr, osend, orecv, fsend, frecv,
-    fr_sem, qs, qr, ns, nr, vs, vr, zs, zr, ps, pr, ks, kr, os, orr, fs, fr,
+    qf_ref, cf_ref,    stage, qland, nland, qall, kbuf, vbuf, vt, sbuf, kft, qfr, osend, orecv, fsend, frecv,
+    st, fr_sem, qs, qr, ns, nr, zs, zr, ks, kr, os, orr, fs, fr,
 ):
     blk, u = lax.axis_index("blk"), lax.axis_index("uly")
     x, z = blk // NZ, lax.rem(blk, NZ)
     me = x * NU + u
     slot = lax.rem(z, 2)
-    lane = pl.multiple_of(slot * HD, HD)
     other = z + 1 - 2 * slot
     base = z - slot
     even = lax.rem(x + z, 2) == 0
@@ -50,11 +49,15 @@
     def along(k):
         return at(x, lax.rem(z + NZ - k, NZ), u)
 
+    staged = [
+        pltpu.make_async_copy(ref, stage.at[i], st.at[i])
+        for i, ref in enumerate((q_ref, kn_ref, vn_ref))
+    ]
     frame_copies = [
         pltpu.make_async_copy(qf_hbm, qf_ref, fr_sem.at[0]),
         pltpu.make_async_copy(cf_hbm, cf_ref, fr_sem.at[1]),
     ]
-    for copy in frame_copies:
+    for copy in staged + frame_copies:
         copy.start()
 
     barrier = pltpu.get_barrier_semaphore()
@@ -63,38 +66,47 @@
         pl.semaphore_signal(barrier, inc=1, device_id=at(px, z, pu), device_id_type=MESH)
     for k in range(1, NZ):
         pl.semaphore_signal(barrier, inc=1, device_id=along(k), device_id_type=MESH)
-    for step in range(1, NX):
-        pl.semaphore_signal(
-            barrier, inc=1, device_id=at(lax.rem(x + step, NX), other, u), device_id_type=MESH
+    for i in range(1, NX * NU):
+        px, pu = plane(i)
+        pl.semaphore_signal(barrier, inc=1, device_id=at(px, other, pu), device_id_type=MESH)
+    pl.semaphore_wait(barrier, 2 * (NX * NU - 1) + NZ - 1)
+    for copy in staged:
+        copy.wait()
+
+    def remote(src, dst, ssem, rsem, px, pz, pu):
+        return pltpu.make_async_remote_copy(
+            src_ref=src,
+            dst_ref=dst,
+            send_sem=ssem,
+            recv_sem=rsem,
+            device_id=at(px, pz, pu),
+            device_id_type=MESH,
         )
-    pl.semaphore_wait(barrier, NX * NU - 1 + NZ - 1 + NX - 1)
-
-    def columns(px, pu):
-        return pl.ds(pl.multiple_of((HEADS * pu + pair_start(px)) * HD, HD), 2 * HD)
-
-    def small(src, dst, ssem, rsem):
-        copies = []
-        for i in range(1, NX * NU):
+
+    def heads(px, pu):
+        return HEADS * pu + pair_start(px)
+
+    sends = []
+    for i in range(1, NX * NU):
+        px, pu = plane(i)
+        src = stage.at[0, pl.ds(heads(px, pu), 2)]
+        sends.append(remote(src, qland.at[:, me], qs.at[i], qr.at[me], px, z, pu))
+    for n, pz in enumerate((z, other)):
+        for i in range(1 - n, NX * NU):
             px, pu = plane(i)
-            copies.append(
-                pltpu.make_async_remote_copy(
-                    src_ref=src.at[:, columns(px, pu)],
-                    dst_ref=dst.at[me],
-                    send_sem=ssem.at[i],
-                    recv_sem=rsem.at[me],
-                    device_id=at(px, z, pu),
-                    device_id_type=MESH,
-                )
-            )
-            copies[-1].start()
-        pltpu.make_async_copy(src.at[:, columns(x, u)], dst.at[me], rsem.at[me]).start()
-        return copies
-
-    def landed(dst, rsem):
-        for i in range(NX * NU):
-            pltpu.make_async_copy(dst.at[i], dst.at[i], rsem.at[i]).wait()
-
-    sends = small(q_ref, qland, qs, qr)
+            src = stage.at[pl.ds(1, 2), heads(px, pu) + lax.rem(pz, 2)]
+            dst = nland.at[slot, :, me]
+            sends.append(remote(src, dst, ns.at[n, i], nr.at[slot, me], px, pz, pu))
+    for copy in sends:
+        copy.start()
+    pltpu.make_async_copy(stage.at[0, pl.ds(heads(x, u), 2)], qland.at[:, me], qr.at[me]).start()
+    pltpu.make_async_copy(
+        stage.at[pl.ds(1, 2), heads(x, u) + slot], nland.at[slot, :, me], nr.at[slot, me]
+    ).start()
+
+    def landed(dst, rsem, count=NX * NU):
+        for i in range(count):
+            pltpu.make_async_copy(dst(i), dst(i), rsem.at[i]).wait()
 
     caches = ((0, kc_ref, kbuf), (1, vc_ref, vbuf))
 
@@ -139,9 +151,6 @@
             buf.at[own_slot, pl.ds(0, CTXB)],
             kr.at[i, own_slot],
         ).start()
-
-    sends += small(kn_ref, nland, ns, nr)
-    sends += small(vn_ref, vland, vs, vr)
 
     for copy in frame_copies:
         copy.wait()
@@ -176,46 +185,23 @@
             wide = jnp.broadcast_to(part[:1].astype(F32), (128, 128))
             kft[block, pl.ds(h * 128, 128), :] = wide.T.astype(jnp.int32)
 
-    landed(qland, qr)
+    landed(lambda i: qland.at[:, i], qr)
     for k in (1, 7, 2, 6, 3, 5, 4):
         pz = lax.rem(z + k, NZ)
-        copy = pltpu.make_async_remote_copy(
-            src_ref=qland.at[:, :, pl.ds(pl.multiple_of(lax.rem(pz, 2) * HD, HD), HD)],
-            dst_ref=qall.at[k],
-            send_sem=zs.at[k],
-            recv_sem=zr.at[k],
-            device_id=at(x, pz, u),
-            device_id_type=MESH,
-        )
+        copy = remote(qland.at[lax.rem(pz, 2)], qall.at[k], zs.at[k], zr.at[k], x, pz, u)
         copy.start()
         sends.append(copy)
-    qall[0] = qland[:, :, pl.ds(lane, HD)]
-
-    landed(nland, nr)
-    landed(vland, vr)
-    lands = ((0, nland, npair, kbuf), (1, vland, vpair, vbuf))
-    for i, land, pair, _ in lands:
-        copy = pltpu.make_async_remote_copy(
-            src_ref=land.at[:, :, pl.ds(pl.multiple_of((1 - slot) * HD, HD), HD)],
-            dst_ref=pair,
-            send_sem=ps.at[i],
-            recv_sem=pr.at[i],
-            device_id=at(x, other, u),
-            device_id_type=MESH,
-        )
-        copy.start()
-        sends.append(copy)
-    for i, _, pair, _ in lands:
-        pltpu.make_async_copy(pair, pair, pr.at[i]).wait()
-
-    def join(dst, xx, mine):
-        for i, land, pair, buf in lands:
+    qall[0] = qland[slot]
+
+    for p in range(2):
+        landed(lambda i: nland.at[p, :, i], nr.at[p])
+
+    def join(dst, xx, p):
+        for i, buf in enumerate((kbuf, vbuf)):
             rows = buf.at[dst, pl.ds(0, CTXB)]
             pltpu.make_async_copy(rows, rows, kr.at[i, dst]).wait()
-            here = land[pl.ds(xx * NU, NU), :, pl.ds(lane, HD)]
-            there = pair[pl.ds(xx * NU, NU)]
-            new = jnp.where(mine, here.astype(F32), there.astype(F32))
-            buf[dst, pl.ds(CTXB, NEWB), :] = new.reshape(NEWB, HD).astype(BF16)
+            new = nland[p, i, pl.ds(xx * NU, NU)].astype(F32).reshape(NEWB, HD)
+            buf[dst, pl.ds(CTXB, NEWB), :] = new.astype(BF16)
         vt[dst] = vbuf[dst].T
 
     def order(i):
@@ -271,7 +257,7 @@
     def work(blocks):
         for dst, block in blocks:
             xx = lax.rem(block, NX)
-            join(dst, xx, block // NX == slot)
+            join(dst, xx, block // NX)
 
         def chunk(i, carry):
             attend(blocks, i)
@@ -308,39 +294,38 @@
         return merged / total, top + jnp.log2(total)
 
     merged, level = merge(1)
-    fsend[:, pl.ds(TOK, TOK), :] = merged.T.reshape(NX * NU, TOK, HD)
-    fsend[:, pl.ds(2 * TOK, TOK), :] = jnp.broadcast_to(level, (128, 128)).T.reshape(
-        NX * NU, TOK, HD
-    )
+    fsend[:, 1] = merged.T.reshape(NX * NU, TOK, HD).astype(BF16)
+    one = level.astype(BF16).astype(F32)
+    two = (level - one).astype(BF16).astype(F32)
+    three = level - one - two
+    row = lax.broadcasted_iota(jnp.int32, (128, 128), 0)
+    level = jnp.where(row == 0, one, jnp.where(row == 1, two, jnp.where(row == 2, three, 0.0)))
+    fsend[:, 2] = level.T.reshape(NX * NU, TOK, HD).astype(BF16)
     merged, _ = merge(0)
-    fsend[:, pl.ds(0, TOK), :] = merged.T.reshape(NX * NU, TOK, HD)
+    fsend[:, 0] = merged.T.reshape(NX * NU, TOK, HD).astype(BF16)
 
     for i in range(1, NX * NU):
         px, pu = plane(i)
-        copy = pltpu.make_async_remote_copy(
-            src_ref=fsend.at[px * NU + pu],
-            dst_ref=frecv.at[me],
-            send_sem=fs.at[i],
-            recv_sem=fr.at[me],
-            device_id=at(px, z, pu),
-            device_id_type=MESH,
-        )
+        copy = remote(fsend.at[px * NU + pu], frecv.at[me], fs.at[i], fr.at[me], px, z, pu)
         copy.start()
         sends.append(copy)
     pltpu.make_async_copy(fsend.at[me], frecv.at[me], fr.at[me]).start()
-    landed(frecv, fr)
+    landed(lambda i: frecv.at[i], fr)
     for uu in range(NU):
         for half in range(2):
             ends = (frecv.at[2 * half * NU + uu], frecv.at[(2 * half + 1) * NU + uu])
-            base = (HEADS * uu + 3 * half) * HD
-            for e, end in enumerate(ends):
-                out_ref[:, pl.ds(base + 2 * e * HD, HD)] = end[pl.ds(0, TOK), :].astype(BF16)
-            levels = [end[pl.ds(2 * TOK, TOK), :] for end in ends]
+            head = HEADS * uu + 3 * half
+            out_ref[head] = ends[0][0]
+            out_ref[head + 2] = ends[1][0]
+            levels = []
+            for end in ends:
+                tail = end[2].astype(F32)
+                levels.append(tail[:, 0:1] + tail[:, 1:2] + tail[:, 2:3])
             top = jnp.maximum(levels[0], levels[1])
             w = [jnp.exp2(level - top) for level in levels]
-            both = [end[pl.ds(TOK, TOK), :] for end in ends]
+            both = [end[1].astype(F32) for end in ends]
             mixed = (both[0] * w[0] + both[1] * w[1]) / (w[0] + w[1])
-            out_ref[:, pl.ds(base + HD, HD)] = mixed.astype(BF16)
+            out_ref[head + 1] = mixed.astype(BF16)
 
     for copy in sends:
         copy.wait_send()
@@ -364,19 +349,21 @@
     vmem = pl.BlockSpec(memory_space=pltpu.VMEM)
     dma = pltpu.SemaphoreType.DMA
     n = NX * NU
-    return pl.pallas_call(
+
+    def by_head(rows):
+        return rows.reshape(TOK, NU * HEADS, HD).transpose(1, 0, 2)
+
+    out = pl.pallas_call(
         kernel,
-        out_shape=jax.ShapeDtypeStruct((TOK, queries.shape[1]), BF16),
+        out_shape=jax.ShapeDtypeStruct((NU * HEADS, TOK, HD), BF16),
         in_specs=[hbm] * 7,
         out_specs=vmem,
         scratch_shapes=[
             pltpu.VMEM((8, 128), jnp.int32),
             pltpu.VMEM((56, 128), jnp.int32),
-            pltpu.VMEM((n, TOK, 2 * HD), BF16),
-            pltpu.VMEM((n, TOK, 2 * HD), BF16),
-            pltpu.VMEM((n, TOK, 2 * HD), BF16),
-            pltpu.VMEM((n, TOK, HD), BF16),
-            pltpu.VMEM((n, TOK, HD), BF16),
+            pltpu.VMEM((3, NU * HEADS, TOK, HD), BF16),
+            pltpu.VMEM((2, n, TOK, HD), BF16),
+            pltpu.VMEM((2, 2, n, TOK, HD), BF16),
             pltpu.VMEM((NZ, n, TOK, HD), BF16),
             pltpu.VMEM((2 * NX, KB, HD), BF16),
             pltpu.VMEM((2 * NX, KB, HD), BF16),
@@ -386,12 +373,12 @@
             pltpu.VMEM((NZ, 8, 128), jnp.int32),
             pltpu.VMEM((NZ, HD + 16, 128), BF16),
             pltpu.VMEM((NZ, HD + 16, 128), BF16),
-            pltpu.VMEM((n, 3 * TOK, HD), F32),
-            pltpu.VMEM((n, 3 * TOK, HD), F32),
-            dma((2,)),
-            dma((n,)), dma((n,)), dma((n,)), dma((n,)), dma((n,)), dma((n,)),
+            pltpu.VMEM((n, 3, TOK, HD), BF16),
+            pltpu.VMEM((n, 3, TOK, HD), BF16),
+            dma((3,)), dma((2,)),
+            dma((n,)), dma((n,)),
+            dma((2, n)), dma((2, n)),
             dma((NZ,)), dma((NZ,)),
-            dma((2,)), dma((2,)),
             dma((2, 2 * NX)), dma((2, 2 * NX)),
             dma((NZ,)), dma((NZ,)),
             dma((n,)), dma((n,)),
@@ -400,9 +387,10 @@
             collective_id=0, has_side_effects=True, vmem_limit_bytes=64 * 2**20
         ),
     )(
-        queries, keys_new, values_new, keys_cache, values_cache,
+        by_head(queries), by_head(keys_new), by_head(values_new), keys_cache, values_cache,
         query_frame.reshape(8, 128), context_frame.reshape(56, 128),
     )
+    return out.transpose(1, 0, 2).reshape(queries.shape)
 
 
 def solution(mesh):

time: 51.9 us -> 46.6 us (0.90)
  Pallas kernels: 50.3 us -> 45.1 us
    pallas_call x1, Pallas kernels: 50.3 us -> 45.1 us  [shards(): pl.pallas_call(kernel, out_shape=jax.ShapeDtypeStruct((NU * HEADS, TOK, H...]
where the time goes in v3:
time: 46.6 us; the launch traced here: 46.5 us
  Pallas kernels  45.1 us (97%)
  local copies, waits for them, and re-layouts  1.42 us (3%)
    pallas_call x1, Pallas kernels, shards(): pl.pallas_call(kernel, out_shape=jax.ShapeDtypeStruct((NU * HEADS, TOK, H...  45.1 us
    unnamed x1, local copies, waits for them, and re-layouts  1.42 us

profile of v3, /device:TPU:1, one launch (start us, length us, event | category | flops | bytes accessed | tf_op | source)
XLA Modules:
  0.0 46.5 jit_solution(6520530194300402078)
XLA Ops:
  0.0 45.1 %shard_map.73 = bf16[24,8,128]{2,1,0:T(8,128)(2,1)} custom-call(bf16[24,8,128]{2,1,0:T(8,128)(2,1)} %bitcast.15, bf16[24,8,128]{2,1,0:T(8,128)(2,1)} %bitcast.16, bf16[24,8,128]{2,1,0:T(8,128)(2,1)} %bitcast.17, bf16[224,768]{1,0:T(8,128)(2,1)} %kc_ref.1, bf16[224,768]{1,0:T(8,128)(2,1)} %vc_ref.1, s32[8,128]{1,0:T(8,128)} %bitcast.19, s32[56,128]{1,0:T(8,128)} %bitcast.18), custom_call_target="tpu_custom_call" | custom-call | tf_op jit(solution)/shard_map/pallas_call | solution.py:356
  45.1 1.4 %copy.9 = bf16[8,3072]{1,0:T(8,128)(2,1)} copy(bf16[8,3072]{1,0:T(8,128)(2,1)} %bitcast.14) | data formatting | bytes 98304

commit v4 on v3

--- a/solution.py
+++ b/solution.py
@@ -27,8 +27,8 @@
 
 def kernel(
     q_ref, kn_ref, vn_ref, kc_ref, vc_ref, qf_hbm, cf_hbm, out_ref,
-    qf_ref, cf_ref,    stage, qland, nland, qall, kbuf, vbuf, vt, sbuf, kft, qfr, osend, orecv, fsend, frecv,
-    st, fr_sem, qs, qr, ns, nr, zs, zr, ks, kr, os, orr, fs, fr,
+    qf_ref, cf_ref,    stage, cache, qland, nland, qall, kvbuf, vt, sbuf, kft, qfr, osend, orecv, fsend, frecv,
+    st, ct, fr_sem, qs, qr, ns, nr, zs, zr, ks, kr, os, orr, fs, fr,
 ):
     blk, u = lax.axis_index("blk"), lax.axis_index("uly")
     x, z = blk // NZ, lax.rem(blk, NZ)
@@ -57,7 +57,12 @@
         pltpu.make_async_copy(qf_hbm, qf_ref, fr_sem.at[0]),
         pltpu.make_async_copy(cf_hbm, cf_ref, fr_sem.at[1]),
     ]
-    for copy in staged + frame_copies:
+    cache_copies = [
+        pltpu.make_async_copy(ref.at[:, pl.ds(h * HD, HD)], cache.at[h, i], ct.at[h, i])
+        for h in range(HEADS)
+        for i, ref in enumerate((kc_ref, vc_ref))
+    ]
+    for copy in staged + cache_copies + frame_copies:
         copy.start()
 
     barrier = pltpu.get_barrier_semaphore()
@@ -108,49 +113,37 @@
         for i in range(count):
             pltpu.make_async_copy(dst(i), dst(i), rsem.at[i]).wait()
 
-    caches = ((0, kc_ref, kbuf), (1, vc_ref, vbuf))
-
     def cached(px, pz, ssem):
-        mine = lax.rem(z, 2)
         whole = lax.rem(px + pz, 2) == 0
-        far = (x != px).astype(jnp.int32)
-        dst = jnp.where(whole, mine * NX + x, mine * 2 + far)
-        copies = []
-        for i, ref, buf in caches:
-            src = ref.at[:, pl.ds(pl.multiple_of((pair_start(px) + lax.rem(pz, 2)) * HD, HD), HD)]
-            copies.append(
-                pltpu.make_async_remote_copy(
-                    src_ref=src,
-                    dst_ref=buf.at[dst, pl.ds(0, CTXB)],
-                    send_sem=ks.at[i, ssem],
-                    recv_sem=kr.at[i, dst],
-                    device_id=at(px, pz, u),
-                    device_id_type=MESH,
-                )
-            )
-        return copies
+        dst = jnp.where(whole, slot * NX + x, x)
+        return remote(
+            cache.at[pair_start(px) + lax.rem(pz, 2)],
+            kvbuf.at[dst, :, pl.ds(0, CTXB)],
+            ks.at[ssem],
+            kr.at[dst],
+            px,
+            pz,
+            u,
+        )
 
     def takes(px, pz):
-        return (lax.rem(px + pz, 2) == 0) | (px == x) | (px == NX - 1 - x)
-
-    for step in (2, 1, 3, 0):
-        px = lax.rem(x + step, NX)
-        for n, pz in enumerate((other, z)):
-            if step == 0 and n == 1:
-                continue
+        return (lax.rem(px + pz, 2) == 0) | (pz == z)
+
+    def to_plane(act, steps, n):
+        for step in steps:
+            px, pz = lax.rem(x + step, NX), (other, z)[n]
 
             @pl.when(takes(px, pz))
             def _():
-                for copy in cached(px, pz, 2 * step + n):
-                    copy.start()
-
-    own_slot = jnp.where(even, slot * NX + x, slot * 2)
-    for i, ref, buf in caches:
-        pltpu.make_async_copy(
-            ref.at[:, pl.ds(pl.multiple_of((pair_start(x) + slot) * HD, HD), HD)],
-            buf.at[own_slot, pl.ds(0, CTXB)],
-            kr.at[i, own_slot],
-        ).start()
+                act(cached(px, pz, 2 * step + n))
+
+    for copy in cache_copies:
+        copy.wait()
+    to_plane(lambda copy: copy.start(), (2, 1, 3, 0), 0)
+    own_slot = jnp.where(even, slot * NX + x, x)
+    pltpu.make_async_copy(
+        cache.at[pair_start(x) + slot], kvbuf.at[own_slot, :, pl.ds(0, CTXB)], kr.at[own_slot]
+    ).start()
 
     for copy in frame_copies:
         copy.wait()
@@ -191,22 +184,23 @@
         copy = remote(qland.at[lax.rem(pz, 2)], qall.at[k], zs.at[k], zr.at[k], x, pz, u)
         copy.start()
         sends.append(copy)
+    to_plane(lambda copy: copy.start(), (2, 1, 3), 1)
     qall[0] = qland[slot]
 
     for p in range(2):
         landed(lambda i: nland.at[p, :, i], nr.at[p])
 
     def join(dst, xx, p):
-        for i, buf in enumerate((kbuf, vbuf)):
-            rows = buf.at[dst, pl.ds(0, CTXB)]
-            pltpu.make_async_copy(rows, rows, kr.at[i, dst]).wait()
+        rows = kvbuf.at[dst, :, pl.ds(0, CTXB)]
+        pltpu.make_async_copy(rows, rows, kr.at[dst]).wait()
+        for i in range(2):
             new = nland[p, i, pl.ds(xx * NU, NU)].astype(F32).reshape(NEWB, HD)
-            buf[dst, pl.ds(CTXB, NEWB), :] = new.astype(BF16)
-        vt[dst] = vbuf[dst].T
+            kvbuf[dst, i, pl.ds(CTXB, NEWB), :] = new.astype(BF16)
+        vt[dst] = kvbuf[dst, 1].T
 
     def order(i):
         odd = lax.rem(i, 2)
-        return odd * ((i + 1) // 2) + (1 - odd) * lax.rem(NZ - i // 2, NZ)
+        return odd * lax.rem(4 + (i + 1) // 2, NZ) + (1 - odd) * (4 - i // 2)
 
     def attend(blocks, i):
         k = order(i)
@@ -221,7 +215,7 @@
         top = jnp.full((8, 128), LOW, F32)
         for dst, block in blocks:
             s = lax.dot_general(
-                kbuf[dst], query, (((1,), (1,)), ((), ())), preferred_element_type=F32
+                kvbuf[dst, 0], query, (((1,), (1,)), ((), ())), preferred_element_type=F32
             )
             s = jnp.where(kft[block] <= frames, s * SCALE, LOW)
             sbuf[dst] = s
@@ -271,7 +265,7 @@
 
     @pl.when(jnp.logical_not(even))
     def _():
-        work([(2 * b + f, b * NX + (x if f == 0 else NX - 1 - x)) for b in range(2) for f in range(2)])
+        work([(b, slot * NX + b) for b in range(NX)])
 
     orecv[0] = osend[0]
 
@@ -329,17 +323,8 @@
 
     for copy in sends:
         copy.wait_send()
-    for step in range(NX):
-        px = lax.rem(x + step, NX)
-        for n, pz in enumerate((other, z)):
-            if step == 0 and n == 1:
-                continue
-
-            @pl.when(takes(px, pz))
-            def _():
-                for copy in cached(px, pz, 2 * step + n):
-                    copy.wait_send()
-
+    to_plane(lambda copy: copy.wait_send(), (2, 1, 3, 0), 0)
+    to_plane(lambda copy: copy.wait_send(), (2, 1, 3), 1)
     for k in range(1, NZ):
         pltpu.make_async_copy(osend.at[k], osend.at[k], os.at[k]).wait()
 
@@ -362,11 +347,11 @@
             pltpu.VMEM((8, 128), jnp.int32),
             pltpu.VMEM((56, 128), jnp.int32),
             pltpu.VMEM((3, NU * HEADS, TOK, HD), BF16),
+            pltpu.VMEM((HEADS, 2, CTXB, HD), BF16),
             pltpu.VMEM((2, n, TOK, HD), BF16),
             pltpu.VMEM((2, 2, n, TOK, HD), BF16),
             pltpu.VMEM((NZ, n, TOK, HD), BF16),
-            pltpu.VMEM((2 * NX, KB, HD), BF16),
-            pltpu.VMEM((2 * NX, KB, HD), BF16),
+            pltpu.VMEM((2 * NX, 2, KB, HD), BF16),
             pltpu.VMEM((2 * NX, HD, KB), BF16),
             pltpu.VMEM((2 * NX, KB, 128), F32),
             pltpu.VMEM((2 * NX, KB, 128), jnp.int32),
@@ -375,11 +360,11 @@
             pltpu.VMEM((NZ, HD + 16, 128), BF16),
             pltpu.VMEM((n, 3, TOK, HD), BF16),
             pltpu.VMEM((n, 3, TOK, HD), BF16),
-            dma((3,)), dma((2,)),
+            dma((3,)), dma((HEADS, 2)), dma((2,)),
             dma((n,)), dma((n,)),
             dma((2, n)), dma((2, n)),
             dma((NZ,)), dma((NZ,)),
-            dma((2, 2 * NX)), dma((2, 2 * NX)),
+            dma((2 * NX,)), dma((2 * NX,)),
             dma((NZ,)), dma((NZ,)),
             dma((n,)), dma((n,)),
         ],

time: 46.6 us -> 45.2 us (0.970)
  Pallas kernels: 45.1 us -> 43.7 us
    pallas_call x1, Pallas kernels: 45.1 us -> 43.7 us  [shards(): pl.pallas_call(kernel, out_shape=jax.ShapeDtypeStruct((NU * HEADS, TOK, H...]
where the time goes in v4:
time: 45.2 us; the launch traced here: 45.1 us
  Pallas kernels  43.7 us (97%)
  local copies, waits for them, and re-layouts  1.42 us (3%)
    pallas_call x1, Pallas kernels, shards(): pl.pallas_call(kernel, out_shape=jax.ShapeDtypeStruct((NU * HEADS, TOK, H...  43.7 us
    unnamed x1, local copies, waits for them, and re-layouts  1.42 us

profile of v4, /device:TPU:1, one launch (start us, length us, event | category | flops | bytes accessed | tf_op | source)
XLA Modules:
  0.0 45.1 jit_solution(1255798612926147794)
XLA Ops:
  0.0 43.7 %shard_map.73 = bf16[24,8,128]{2,1,0:T(8,128)(2,1)} custom-call(bf16[24,8,128]{2,1,0:T(8,128)(2,1)} %bitcast.15, bf16[24,8,128]{2,1,0:T(8,128)(2,1)} %bitcast.16, bf16[24,8,128]{2,1,0:T(8,128)(2,1)} %bitcast.17, bf16[224,768]{1,0:T(8,128)(2,1)} %kc_ref.1, bf16[224,768]{1,0:T(8,128)(2,1)} %vc_ref.1, s32[8,128]{1,0:T(8,128)} %bitcast.19, s32[56,128]{1,0:T(8,128)} %bitcast.18), custom_call_target="tpu_custom_call" | custom-call | tf_op jit(solution)/shard_map/pallas_call | solution.py:341
  43.7 1.4 %copy.9 = bf16[8,3072]{1,0:T(8,128)(2,1)} copy(bf16[8,3072]{1,0:T(8,128)(2,1)} %bitcast.14) | data formatting | bytes 98304

commit v5 on v4

--- a/solution.py
+++ b/solution.py
@@ -27,7 +27,7 @@
 
 def kernel(
     q_ref, kn_ref, vn_ref, kc_ref, vc_ref, qf_hbm, cf_hbm, out_ref,
-    qf_ref, cf_ref,    stage, cache, qland, nland, qall, kvbuf, vt, sbuf, kft, qfr, osend, orecv, fsend, frecv,
+    qf_ref, cf_ref,    qstage, nstage, cache, qland, qz, nland, qall, kvbuf, vt, sbuf, kft, qfr, osend, orecv, fsend, frecv,
     st, ct, fr_sem, qs, qr, ns, nr, zs, zr, ks, kr, os, orr, fs, fr,
 ):
     blk, u = lax.axis_index("blk"), lax.axis_index("uly")
@@ -50,8 +50,9 @@
         return at(x, lax.rem(z + NZ - k, NZ), u)
 
     staged = [
-        pltpu.make_async_copy(ref, stage.at[i], st.at[i])
-        for i, ref in enumerate((q_ref, kn_ref, vn_ref))
+        pltpu.make_async_copy(q_ref, qstage, st.at[0]),
+        pltpu.make_async_copy(kn_ref, nstage.at[:, 0], st.at[1]),
+        pltpu.make_async_copy(vn_ref, nstage.at[:, 1], st.at[2]),
     ]
     frame_copies = [
         pltpu.make_async_copy(qf_hbm, qf_ref, fr_sem.at[0]),
@@ -74,77 +75,6 @@
     for i in range(1, NX * NU):
         px, pu = plane(i)
         pl.semaphore_signal(barrier, inc=1, device_id=at(px, other, pu), device_id_type=MESH)
-    pl.semaphore_wait(barrier, 2 * (NX * NU - 1) + NZ - 1)
-    for copy in staged:
-        copy.wait()
-
-    def remote(src, dst, ssem, rsem, px, pz, pu):
-        return pltpu.make_async_remote_copy(
-            src_ref=src,
-            dst_ref=dst,
-            send_sem=ssem,
-            recv_sem=rsem,
-            device_id=at(px, pz, pu),
-            device_id_type=MESH,
-        )
-
-    def heads(px, pu):
-        return HEADS * pu + pair_start(px)
-
-    sends = []
-    for i in range(1, NX * NU):
-        px, pu = plane(i)
-        src = stage.at[0, pl.ds(heads(px, pu), 2)]
-        sends.append(remote(src, qland.at[:, me], qs.at[i], qr.at[me], px, z, pu))
-    for n, pz in enumerate((z, other)):
-        for i in range(1 - n, NX * NU):
-            px, pu = plane(i)
-            src = stage.at[pl.ds(1, 2), heads(px, pu) + lax.rem(pz, 2)]
-            dst = nland.at[slot, :, me]
-            sends.append(remote(src, dst, ns.at[n, i], nr.at[slot, me], px, pz, pu))
-    for copy in sends:
-        copy.start()
-    pltpu.make_async_copy(stage.at[0, pl.ds(heads(x, u), 2)], qland.at[:, me], qr.at[me]).start()
-    pltpu.make_async_copy(
-        stage.at[pl.ds(1, 2), heads(x, u) + slot], nland.at[slot, :, me], nr.at[slot, me]
-    ).start()
-
-    def landed(dst, rsem, count=NX * NU):
-        for i in range(count):
-            pltpu.make_async_copy(dst(i), dst(i), rsem.at[i]).wait()
-
-    def cached(px, pz, ssem):
-        whole = lax.rem(px + pz, 2) == 0
-        dst = jnp.where(whole, slot * NX + x, x)
-        return remote(
-            cache.at[pair_start(px) + lax.rem(pz, 2)],
-            kvbuf.at[dst, :, pl.ds(0, CTXB)],
-            ks.at[ssem],
-            kr.at[dst],
-            px,
-            pz,
-            u,
-        )
-
-    def takes(px, pz):
-        return (lax.rem(px + pz, 2) == 0) | (pz == z)
-
-    def to_plane(act, steps, n):
-        for step in steps:
-            px, pz = lax.rem(x + step, NX), (other, z)[n]
-
-            @pl.when(takes(px, pz))
-            def _():
-                act(cached(px, pz, 2 * step + n))
-
-    for copy in cache_copies:
-        copy.wait()
-    to_plane(lambda copy: copy.start(), (2, 1, 3, 0), 0)
-    own_slot = jnp.where(even, slot * NX + x, x)
-    pltpu.make_async_copy(
-        cache.at[pair_start(x) + slot], kvbuf.at[own_slot, :, pl.ds(0, CTXB)], kr.at[own_slot]
-    ).start()
-
     for copy in frame_copies:
         copy.wait()
     lanes = lax.broadcasted_iota(jnp.int32, (1, 128), 1)
@@ -178,23 +108,103 @@
             wide = jnp.broadcast_to(part[:1].astype(F32), (128, 128))
             kft[block, pl.ds(h * 128, 128), :] = wide.T.astype(jnp.int32)
 
-    landed(lambda i: qland.at[:, i], qr)
-    for k in (1, 7, 2, 6, 3, 5, 4):
+    pl.semaphore_wait(barrier, 2 * (NX * NU - 1) + NZ - 1)
+    for copy in staged:
+        copy.wait()
+
+    def remote(src, dst, ssem, rsem, px, pz, pu):
+        return pltpu.make_async_remote_copy(
+            src_ref=src,
+            dst_ref=dst,
+            send_sem=ssem,
+            recv_sem=rsem,
+            device_id=at(px, pz, pu),
+            device_id_type=MESH,
+        )
+
+    def heads(px, pu):
+        return HEADS * pu + pair_start(px)
+
+    sends = []
+    for i in range(1, NX * NU):
+        px, pu = plane(i)
+        src = qstage.at[pl.ds(heads(px, pu), 2)]
+        sends.append(remote(src, qland.at[me], qs.at[i], qr.at[me], px, z, pu))
+    for n, pz in enumerate((z, other)):
+        for i in range(1 - n, NX * NU):
+            px, pu = plane(i)
+            src = nstage.at[heads(px, pu) + lax.rem(pz, 2)]
+            dst = nland.at[slot, me]
+            sends.append(remote(src, dst, ns.at[n, i], nr.at[slot, me], px, pz, pu))
+    def go(copies):
+        for copy in copies:
+            copy.start()
+
+    n = NX * NU
+    group, new_here, new_other = sends[: n - 1], sends[n - 1 : 2 * n - 2], sends[2 * n - 2 :]
+    go(group)
+    go(new_other)
+    pltpu.make_async_copy(qstage.at[pl.ds(heads(x, u), 2)], qland.at[me], qr.at[me]).start()
+    pltpu.make_async_copy(
+        nstage.at[heads(x, u) + slot], nland.at[slot, me], nr.at[slot, me]
+    ).start()
+
+    def landed(dst, rsem, count=NX * NU):
+        for i in range(count):
+            pltpu.make_async_copy(dst(i), dst(i), rsem.at[i]).wait()
+
+    def cached(px, pz, ssem):
+        whole = lax.rem(px + pz, 2) == 0
+        dst = jnp.where(whole, slot * NX + x, x)
+        return remote(
+            cache.at[pair_start(px) + lax.rem(pz, 2)],
+            kvbuf.at[dst, :, pl.ds(0, CTXB)],
+            ks.at[ssem],
+            kr.at[dst],
+            px,
+            pz,
+            u,
+        )
+
+    def takes(px, pz):
+        return (lax.rem(px + pz, 2) == 0) | (pz == z)
+
+    def to_plane(act, steps, n):
+        for step in steps:
+            px, pz = lax.rem(x + step, NX), (other, z)[n]
+
+            @pl.when(takes(px, pz))
+            def _():
+                act(cached(px, pz, 2 * step + n))
+
+    for copy in cache_copies:
+        copy.wait()
+    to_plane(lambda copy: copy.start(), (2, 1, 3, 0), 0)
+    go(new_here)
+    own_slot = jnp.where(even, slot * NX + x, x)
+    pltpu.make_async_copy(
+        cache.at[pair_start(x) + slot], kvbuf.at[own_slot, :, pl.ds(0, CTXB)], kr.at[own_slot]
+    ).start()
+
+    landed(lambda i: qland.at[i], qr)
+    for h in range(2):
+        qz[h] = qland[:, h]
+    for k in (4, 3, 5, 2, 6, 1, 7):
         pz = lax.rem(z + k, NZ)
-        copy = remote(qland.at[lax.rem(pz, 2)], qall.at[k], zs.at[k], zr.at[k], x, pz, u)
+        copy = remote(qz.at[lax.rem(pz, 2)], qall.at[k], zs.at[k], zr.at[k], x, pz, u)
         copy.start()
         sends.append(copy)
     to_plane(lambda copy: copy.start(), (2, 1, 3), 1)
-    qall[0] = qland[slot]
+    qall[0] = qz[slot]
 
     for p in range(2):
-        landed(lambda i: nland.at[p, :, i], nr.at[p])
+        landed(lambda i: nland.at[p, i], nr.at[p])
 
     def join(dst, xx, p):
         rows = kvbuf.at[dst, :, pl.ds(0, CTXB)]
         pltpu.make_async_copy(rows, rows, kr.at[dst]).wait()
         for i in range(2):
-            new = nland[p, i, pl.ds(xx * NU, NU)].astype(F32).reshape(NEWB, HD)
+            new = nland[p, pl.ds(xx * NU, NU), i].astype(F32).reshape(NEWB, HD)
             kvbuf[dst, i, pl.ds(CTXB, NEWB), :] = new.astype(BF16)
         vt[dst] = kvbuf[dst, 1].T
 
@@ -346,10 +356,12 @@
         scratch_shapes=[
             pltpu.VMEM((8, 128), jnp.int32),
             pltpu.VMEM((56, 128), jnp.int32),
-            pltpu.VMEM((3, NU * HEADS, TOK, HD), BF16),
+            pltpu.VMEM((NU * HEADS, TOK, HD), BF16),
+            pltpu.VMEM((NU * HEADS, 2, TOK, HD), BF16),
             pltpu.VMEM((HEADS, 2, CTXB, HD), BF16),
+            pltpu.VMEM((n, 2, TOK, HD), BF16),
             pltpu.VMEM((2, n, TOK, HD), BF16),
-            pltpu.VMEM((2, 2, n, TOK, HD), BF16),
+            pltpu.VMEM((2, n, 2, TOK, HD), BF16),
             pltpu.VMEM((NZ, n, TOK, HD), BF16),
             pltpu.VMEM((2 * NX, 2, KB, HD), BF16),
             pltpu.VMEM((2 * NX, HD, KB), BF16),

time: 45.2 us -> 44.9 us (level)
  Pallas kernels: 43.7 us -> 43.2 us
    pallas_call x1, Pallas kernels: 43.7 us -> 43.2 us  [shards(): pl.pallas_call(kernel, out_shape=jax.ShapeDtypeStruct((NU * HEADS, TOK, H...]
where the time goes in v5:
time: 44.9 us; the launch traced here: 44.7 us
  Pallas kernels  43.2 us (96%)
  local copies, waits for them, and re-layouts  1.42 us (3%)
    pallas_call x1, Pallas kernels, shards(): pl.pallas_call(kernel, out_shape=jax.ShapeDtypeStruct((NU * HEADS, TOK, H...  43.2 us
    unnamed x1, local copies, waits for them, and re-layouts  1.42 us

profile of v5, /device:TPU:1, one launch (start us, length us, event | category | flops | bytes accessed | tf_op | source)
XLA Modules:
  0.0 44.7 jit_solution(9476358768796717935)
XLA Ops:
  0.0 43.2 %shard_map.73 = bf16[24,8,128]{2,1,0:T(8,128)(2,1)} custom-call(bf16[24,8,128]{2,1,0:T(8,128)(2,1)} %bitcast.15, bf16[24,8,128]{2,1,0:T(8,128)(2,1)} %bitcast.16, bf16[24,8,128]{2,1,0:T(8,128)(2,1)} %bitcast.17, bf16[224,768]{1,0:T(8,128)(2,1)} %kc_ref.1, bf16[224,768]{1,0:T(8,128)(2,1)} %vc_ref.1, s32[8,128]{1,0:T(8,128)} %bitcast.19, s32[56,128]{1,0:T(8,128)} %bitcast.18), custom_call_target="tpu_custom_call" | custom-call | tf_op jit(solution)/shard_map/pallas_call | solution.py:351
  43.2 1.4 %copy.9 = bf16[8,3072]{1,0:T(8,128)(2,1)} copy(bf16[8,3072]{1,0:T(8,128)(2,1)} %bitcast.14) | data formatting | bytes 98304
